TPU v7x, 32 devices: a whole 2x2x4 slice. The times are simulated.
32 devices in a mesh: row: 8 (over z, x), col: 4 (over y, core).
Axes of the slice: x: 2, y: 2, z: 4, core: 2. Of those that a mesh axis runs over, the one named last changes fastest.
Arguments:
- src_points: bfloat16 [128, 64, 1024], P('row', 'col'), may hold values from -1.5 to 1.5
- dst_points: bfloat16 [16, 64, 1024], P('col', 'row'), may hold values from -1.5 to 1.5
- support: int32 [128, 8], P('row'), may hold values from 0 to 15, as said below
- log_src_mass: float32 [128, 1024], P('row'), may hold values from -1 to 1
- log_dst_mass: float32 [16, 1024], P('col'), may hold values from -1 to 1
- dst_potential: float32 [16, 1024], P('col'), may hold values from -4 to 114
Outputs:
- src_potential_new: float32 [128, 1024], P('row')
- dst_potential_new: float32 [16, 1024], P('col')
Inputs may be any that keep to these rules, and one draw needn't show every extreme that they name: `support`: each row cluster names 8 different column clusters; column cluster b belongs to col index b // 4; the col indices that one row cluster names lie in 3 cyclically consecutive indices of col, each of them named at least once; every column cluster is named by some row cluster; for every index of row and every index of col, at most 12 of the 16 row clusters of that row index name a column cluster of that col index, and some pair reaches 12.
All inputs are finite; a program needn't handle non-finite values.
Results may differ from a plain program's by a relative error of at most 0.0003.
Values may be sent and summed in bfloat16 or wider, within the bound.
A program may use at most 64 MiB of HBM per device.

v0:
```python
import jax
import jax.numpy as jnp
from jax import lax
from jax.sharding import PartitionSpec as P

blur_scale = 0.5
floor_value = -1e30


def combine_parts(first_part, second_part):
    highest = jnp.maximum(first_part[0], second_part[0])
    totals = first_part[1] * jnp.exp(first_part[0] - highest) + second_part[1] * jnp.exp(
        second_part[0] - highest
    )
    return (highest, totals)


def tile_cost(src_full, dst_full, src_sq, dst_sq, row_id, col_id):
    left_side = lax.dynamic_index_in_dim(src_full, row_id, 0, keepdims=False)
    right_side = lax.dynamic_index_in_dim(dst_full, col_id, 0, keepdims=False)
    inner_prod = lax.dot_general(
        left_side, right_side, (((0,), (0,)), ((), ())), preferred_element_type=jnp.float32
    )
    left_sq = lax.dynamic_index_in_dim(src_sq, row_id, 0, keepdims=False)
    right_sq = lax.dynamic_index_in_dim(dst_sq, col_id, 0, keepdims=False)
    return left_sq[:, None] + right_sq[None, :] - 2.0 * inner_prod


def body(src_points, dst_points, support, log_src_mass, log_dst_mass, dst_potential):
    col_count = dst_points.shape[0]
    row_count = support.shape[0]
    per_row = support.shape[1]
    src_full = lax.all_gather(src_points, "col", axis=1, tiled=True)
    row_slot = jnp.arange(row_count, dtype=jnp.int32)
    dst_full = lax.all_gather(dst_points, "row", axis=1, tiled=True)
    src_vals = src_full.astype(jnp.float32)
    dst_vals = dst_full.astype(jnp.float32)
    src_sq = jnp.sum(src_vals * src_vals, axis=1)
    dst_sq = jnp.sum(dst_vals * dst_vals, axis=1)
    col_offset = lax.axis_index("col") * col_count
    chosen = support.reshape(-1)
    is_local = chosen // col_count == lax.axis_index("col")
    local_count = jnp.sum(is_local.astype(jnp.int32))
    sort_keys = jnp.where(is_local, 0, 1).astype(jnp.int32)
    entries = jnp.argsort(sort_keys, stable=True)

    def row_turn(turn_index, running):
        row_high, row_sum = running
        entry_id = entries[turn_index]
        row_id = entry_id // per_row
        col_id = chosen[entry_id] - col_offset
        costs = tile_cost(src_full, dst_full, src_sq, dst_sq, row_slot[row_id], col_id)
        potential = lax.dynamic_index_in_dim(dst_potential, col_id, 0, keepdims=False)
        scores = (potential[None, :] - costs) / blur_scale
        tile_high = jnp.max(scores, axis=1)
        tile_sum = jnp.sum(jnp.exp(scores - tile_high[:, None]), axis=1)
        old_high = lax.dynamic_index_in_dim(row_high, row_id, 0, keepdims=False)
        old_sum = lax.dynamic_index_in_dim(row_sum, row_id, 0, keepdims=False)
        new_high, new_sum = combine_parts((old_high, old_sum), (tile_high, tile_sum))
        row_high = lax.dynamic_update_index_in_dim(row_high, new_high, row_id, 0)
        row_sum = lax.dynamic_update_index_in_dim(row_sum, new_sum, row_id, 0)
        return (row_high, row_sum)

    row_start = (
        jnp.full(log_src_mass.shape, floor_value, jnp.float32),
        jnp.zeros(log_src_mass.shape, jnp.float32),
    )
    row_high, row_sum = lax.fori_loop(0, local_count, row_turn, row_start)
    whole_high = lax.pmax(row_high, "col")
    whole_sum = lax.psum(row_sum * jnp.exp(row_high - whole_high), "col")
    src_new = blur_scale * (log_src_mass - (whole_high + jnp.log(whole_sum)))

    def col_turn(turn_index, running):
        col_high, col_sum = running
        entry_id = entries[turn_index]
        row_id = entry_id // per_row
        col_id = chosen[entry_id] - col_offset
        costs = tile_cost(src_full, dst_full, src_sq, dst_sq, row_slot[row_id], col_id)
        potential = lax.dynamic_index_in_dim(src_new, row_id, 0, keepdims=False)
        scores = (potential[:, None] - costs) / blur_scale
        tile_high = jnp.max(scores, axis=0)
        tile_sum = jnp.sum(jnp.exp(scores - tile_high[None, :]), axis=0)
        old_high = lax.dynamic_index_in_dim(col_high, col_id, 0, keepdims=False)
        old_sum = lax.dynamic_index_in_dim(col_sum, col_id, 0, keepdims=False)
        new_high, new_sum = combine_parts((old_high, old_sum), (tile_high, tile_sum))
        col_high = lax.dynamic_update_index_in_dim(col_high, new_high, col_id, 0)
        col_sum = lax.dynamic_update_index_in_dim(col_sum, new_sum, col_id, 0)
        return (col_high, col_sum)

    col_start = (
        jnp.full(log_dst_mass.shape, floor_value, jnp.float32),
        jnp.zeros(log_dst_mass.shape, jnp.float32),
    )
    col_high, col_sum = lax.fori_loop(0, local_count, col_turn, col_start)
    final_high = lax.pmax(col_high, "row")
    final_sum = lax.psum(col_sum * jnp.exp(col_high - final_high), "row")
    dst_new = blur_scale * (log_dst_mass - (final_high + jnp.log(final_sum)))
    return (src_new, dst_new)


def solution(mesh):
    return jax.shard_map(
        body,
        mesh=mesh,
        in_specs=(
            P("row", "col", None),
            P("col", "row", None),
            P("row", None),
            P("row", None),
            P("col", None),
            P("col", None),
        ),
        out_specs=(P("row", None), P("col", None)),
        check_vma=False,
    )
```

profile of v0, /device:TPU:0, one launch (start us, length us, event | category | flops | bytes accessed | tf_op | source)
XLA Modules:
  0.0 1442.2 jit_solution(6999247910115343915)
XLA Ops:
  8.8 2.5 sort.17
  12.8 33.3 %all_gather.7 = bf16[4,64,1024]{2,1,0:T(8,128)(2,1)S(1)} all-gather(bf16[4,8,1024]{2,1,0:T(8,128)(2,1)} %param.11), channel_id=1, replica_groups=mesh['row'=8,'col'=4] {'row'}, dimensions={1}, use_global_device_ids=true | all-gather | bytes 589824 | tf_op jit(solution)/shard_map/all_gather | solution.py:35
  46.3 2.1 multiply_reduce_fusion
  48.4 647.5 %while.28 = (s32[]{:T(128)}, f32[16,1024]{1,0:T(8,128)S(1)}, f32[16,1024]{1,0:T(8,128)S(1)}, s32[]{:T(128)}, s32[128]{0:T(128)S(1)}, /*index=5*/s32[128]{0:T(128...) while((s32[]{:T(128)}, f32[16,1024]{1,0:T(8,128)S(1)}, ...), condition=%wide.region_7.8_spmd, body=%wide.region_4.7_spmd.sunk | while | flops 147853344 | bytes 8753732 | solution.py:68
  71.9 2.1 fusion.19
  140.7 2.1 fusion.19
  154.4 2.1 fusion.19
  209.5 2.1 fusion.19
  223.2 2.1 fusion.19
  250.8 2.1 fusion.19
  278.3 2.1 fusion.19
  292.1 2.1 fusion.19
  319.6 2.1 fusion.19
  347.1 2.1 fusion.19
  415.9 2.1 fusion.19
  484.7 2.1 fusion.19
  553.5 2.1 fusion.19
  622.3 2.1 fusion.19
  691.1 2.1 fusion.19
  696.7 28.5 %all-reduce.3.cloned.1.call-done = f32[16,1024]{1,0:T(8,128)} async-done(((f32[16,1024]{1,0:T(8,128)}), f32[16,1024]{1,0:T(8,128)}) %all-reduce.3.cloned.1.call-update) | async-done | bytes 65552 | tf_op jit(solution)/shard_map/pmax | solution.py:69
  726.7 32.6 %all-reduce.5.cloned.1.call-done = f32[16,1024]{1,0:T(8,128)} async-done(((f32[16,1024]{1,0:T(8,128)}), f32[16,1024]{1,0:T(8,128)}) %all-reduce.5.cloned.1.call-update) | async-done | bytes 65552 | tf_op jit(solution)/shard_map/psum | solution.py:70
  760.2 607.4 %while.29 = (s32[]{:T(128)}, f32[4,1024]{1,0:T(4,128)S(1)}, f32[4,1024]{1,0:T(4,128)S(1)}, s32[]{:T(128)}, s32[128]{0:T(128)S(1)}, /*index=5*/s32[128]{0:T(128)S...) while((s32[]{:T(128)}, f32[4,1024]{1,0:T(4,128)S(1)}, ...), condition=%wide.region_13.14_spmd, body=%wide.region_10.13_spmd.sunk | while | flops 147853344 | bytes 8753732 | solution.py:94
  1367.7 34.3 %pmax.15 = f32[4,1024]{1,0:T(4,128)S(1)} all-reduce(f32[4,1024]{1,0:T(4,128)S(1)} %get-tuple-element.338), channel_id=1, replica_groups=mesh['row'=8,'col'=4] {'row'}, use_global_device_ids=true, to_apply=%region_14.15 | all-reduce | flops 4096 | bytes 32768 | tf_op jit(solution)/shard_map/pmax | solution.py:95
  1402.0 33.0 %psum.15 = f32[4,1024]{1,0:T(4,128)S(1)} all-reduce(f32[4,1024]{1,0:T(4,128)S(1)} %exponential_multiply_fusion.1), channel_id=1, replica_groups=mesh['row'=8,'col'=4] {'row'}, use_global_device_ids=true, to_apply=%region_15.16 | all-reduce | flops 4096 | bytes 32768 | tf_op jit(solution)/shard_map/psum | solution.py:96
  (956 shorter events, 556.2 us)
Async XLA Ops:
  7.2 39.1 %all-gather.2.cloned.1.call-start = ((), (), s32[]{:S(2)}) async-start(), calls=%async_computation | async-start | bytes 2621440 | tf_op jit(solution)/shard_map/all_gather | solution.py:33
  7.9 717.3 %all-reduce.3.cloned.1.call-start = ((), (), s32[]{:S(2)}) async-start(), calls=%async_computation.1 | async-start | bytes 131072 | tf_op jit(solution)/shard_map/pmax | solution.py:69
  48.4 710.9 %copy-start.2 = (f32[16,1024]{1,0:T(8,128)S(1)}, f32[16,1024]{1,0:T(8,128)}, u32[]{:S(2)}) copy-start(f32[16,1024]{1,0:T(8,128)} %param.13) | copy-start | bytes 196612
  696.0 0.6 copy-start
  696.6 62.7 %all-reduce.5.cloned.1.call-start = ((), (), s32[]{:S(2)}) async-start(), calls=%async_computation.2 | async-start | bytes 131072 | tf_op jit(solution)/shard_map/psum | solution.py:70
  760.2 674.8 %copy-start.3 = (f32[4,1024]{1,0:T(4,128)S(1)}, f32[4,1024]{1,0:T(4,128)}, u32[]{:S(2)}) copy-start(f32[4,1024]{1,0:T(4,128)} %param.14) | copy-start | bytes 49156
  1367.7 68.0 %copy-start.1 = (f32[16,1024]{1,0:T(8,128)}, f32[16,1024]{1,0:T(8,128)S(1)}, u32[]{:S(2)}) copy-start(f32[16,1024]{1,0:T(8,128)S(1)} %get-tuple-element.729) | copy-start | bytes 196612
Sparse Core Ops, SparseCore 0:
  9.6 25.2 all-gather.1
  696.7 28.3 all-reduce.2
  728.2 31.0 all-reduce.4
where the time goes:
time: 1470 us; the launch traced here: 1440 us
  loops' own time  675 us (46%)
  local copies, waits for them, and re-layouts  221 us (15%)
  matrix products  190 us (13%)
  other arithmetic  180 us (12%)
  blocking collectives  101 us (7%)
  waiting for transfers between devices  61.8 us (4%)
    another operation x1, loops' own time, body(): col_high, col_sum = lax.fori_loop(0, local_count, col_turn, col_start)  337 us
    another operation x1, loops' own time, body(): row_high, row_sum = lax.fori_loop(0, local_count, row_turn, row_start)  337 us
    dot_general x94, matrix products, tile_cost(): lax.dot_general(left_side, right_side, (((0,), (0,)), ((), ())), preferre...  190 us
    reduce_sum x47, other arithmetic, col_turn(): tile_sum = jnp.sum(jnp.exp(scores - tile_high[None, :]), axis=0)  84.3 us
    reduce_sum x47, other arithmetic, row_turn(): tile_sum = jnp.sum(jnp.exp(scores - tile_high[:, None]), axis=1)  83.4 us
    pmax x1, blocking collectives, body(): final_high = lax.pmax(col_high, 'row')  34.3 us
    dynamic_slice x47, local copies, waits for them, and re-layouts, row_turn(): lax.dynamic_index_in_dim(dst_potential, col_id, 0, keepdims=False)  34.3 us
    all_gather x1, blocking collectives, body(): dst_full = lax.all_gather(dst_points, 'row', axis=1, tiled=True)  33.3 us
  transfers between devices with their start and end apart: 3, of which 2 were waited for; matrix products, arithmetic and copies ran while one was open for 0% of the time, Pallas kernels for 0%

commit v1 on v0

v1 whole, which is shorter than its diff:
```python
import functools

import jax
import jax.numpy as jnp
from jax import lax
from jax.experimental import pallas as pl
from jax.experimental.pallas import tpu as pltpu
from jax.sharding import PartitionSpec as P

blur_scale = 0.5
floor_value = -1e30
row_low, row_top = 1e-6, 1e30
col_low, col_top = 1e-20, 1e20
AUG = 80
ROWS = 256
COLS = 256


def tile_kernel(
    per_dev, sup_ref, x_ref, y_ref, g_ref, mass_ref, src_ref, t_ref, yaug, xt, ebuf, acc
):
    cc, dim, pts = y_ref.shape
    per_row = sup_ref.shape[1]
    first = lax.axis_index("col") * per_dev

    def prep(b, carry):
        y = y_ref[b]
        yf = y.astype(jnp.float32)
        sq = jnp.sum(yf * yf, axis=0, keepdims=True)
        bias = 2.0 * (g_ref[pl.ds(b, 1), :] - sq)
        hi = bias.astype(jnp.bfloat16).astype(jnp.float32)
        rest = bias - hi
        mid = rest.astype(jnp.bfloat16).astype(jnp.float32)
        lo = rest - mid
        at = lax.broadcasted_iota(jnp.int32, (AUG - dim, pts), 0)
        extra = jnp.where(at == 0, hi, jnp.where(at == 1, mid, jnp.where(at == 2, lo, 0.0)))
        yaug[b, :dim, :] = y
        yaug[b, dim:, :] = extra.astype(jnp.bfloat16)
        return carry

    lax.fori_loop(0, cc, prep, 0)
    t_ref[...] = jnp.zeros_like(t_ref)

    def cluster(a, carry):
        xf = x_ref[a].astype(jnp.float32)
        x_sq = jnp.sum(xf * xf, axis=0, keepdims=True)
        at = lax.broadcasted_iota(jnp.int32, (128 - dim, pts), 0)
        whole = jnp.concatenate([xf * 4.0, jnp.where(at < 3, 1.0, 0.0)], axis=0)
        xt[...] = whole.T.astype(jnp.bfloat16)
        acc[...] = jnp.zeros_like(acc)

        def block(k, carry):
            b = sup_ref[first + a, k]
            for n in range(pts // COLS):
                y = yaug[b, :, n * COLS : (n + 1) * COLS]
                for m in range(pts // ROWS):
                    rows = pl.ds(m * ROWS, ROWS)
                    p = jnp.dot(xt[rows, :AUG], y, preferred_element_type=jnp.float32)
                    e = jnp.exp(p)
                    part = e[:, :128]
                    for q in range(1, COLS // 128):
                        part = part + e[:, q * 128 : (q + 1) * 128]
                    acc[rows, :] += part
                    ebuf[k, rows, n * COLS : (n + 1) * COLS] = e.astype(jnp.bfloat16)
            return carry

        lax.fori_loop(0, per_row, block, 0)
        total = jnp.sum(acc[...].T, axis=0, keepdims=True)
        mass = mass_ref[pl.ds(first + a, 1), :]
        src_ref[pl.ds(a, 1), :] = blur_scale * (mass + 2.0 * x_sq - jnp.log(total))
        fine = (total >= row_low) & (total <= row_top)
        w = jnp.where(fine, jnp.exp(mass) / total, jnp.nan)
        w_hi = w.astype(jnp.bfloat16).astype(jnp.float32)
        at16 = lax.broadcasted_iota(jnp.int32, (16, pts), 0)
        w16 = jnp.where(at16 == 0, w_hi, jnp.where(at16 == 1, w - w_hi, 0.0)).astype(jnp.bfloat16)

        def column(k, carry):
            b = sup_ref[first + a, k]
            got = jnp.dot(w16, ebuf[k], preferred_element_type=jnp.float32)
            t_ref[pl.ds(b, 1), :] += got[0:1] + got[1:2]
            return carry

        lax.fori_loop(0, per_row, column, 0)
        return carry

    lax.fori_loop(0, per_dev, cluster, 0)


def tiles(per_dev, support, x_mine, y_all, g_all, log_src_mass):
    cc, dim, pts = y_all.shape
    per_row = support.shape[1]
    vmem = pl.BlockSpec(memory_space=pltpu.VMEM)
    return pl.pallas_call(
        functools.partial(tile_kernel, per_dev),
        out_shape=(
            jax.ShapeDtypeStruct((per_dev, pts), jnp.float32),
            jax.ShapeDtypeStruct((cc, pts), jnp.float32),
        ),
        in_specs=[pl.BlockSpec(memory_space=pltpu.SMEM), vmem, vmem, vmem, vmem],
        out_specs=(vmem, vmem),
        scratch_shapes=[
            pltpu.VMEM((cc, AUG, pts), jnp.bfloat16),
            pltpu.VMEM((pts, 128), jnp.bfloat16),
            pltpu.VMEM((per_row, pts, pts), jnp.bfloat16),
            pltpu.VMEM((pts, 128), jnp.float32),
        ],
        compiler_params=pltpu.CompilerParams(vmem_limit_bytes=56 * 1024 * 1024),
        name="tiles",
    )(support, x_mine, y_all, g_all, log_src_mass)


def exact_path(per_dev, support, x_mine, y_all, g_all, log_src_mass, log_dst_mass):
    cc, dim, pts = y_all.shape
    per_row = support.shape[1]
    first = lax.axis_index("col") * per_dev
    chosen = lax.dynamic_slice_in_dim(support, first, per_dev, 0)
    mass = lax.dynamic_slice_in_dim(log_src_mass, first, per_dev, 0)

    def scores_of(a, b):
        x = lax.dynamic_index_in_dim(x_mine, a, 0, keepdims=False)
        y = lax.dynamic_index_in_dim(y_all, b, 0, keepdims=False)
        xf, yf = x.astype(jnp.float32), y.astype(jnp.float32)
        inner = lax.dot_general(x, y, (((0,), (0,)), ((), ())), preferred_element_type=jnp.float32)
        return jnp.sum(xf * xf, 0)[:, None] + jnp.sum(yf * yf, 0)[None, :] - 2.0 * inner

    def row_turn(t, running):
        high, total = running
        a, b = t // per_row, chosen[t // per_row, t % per_row]
        s = (g_all[b][None, :] - scores_of(a, b)) / blur_scale
        new_high = jnp.maximum(high[a], jnp.max(s, axis=1))
        new_total = total[a] * jnp.exp(high[a] - new_high) + jnp.sum(
            jnp.exp(s - new_high[:, None]), axis=1
        )
        return high.at[a].set(new_high), total.at[a].set(new_total)

    start = (jnp.full((per_dev, pts), floor_value), jnp.zeros((per_dev, pts)))
    high, total = lax.fori_loop(0, per_dev * per_row, row_turn, start)
    src_mine = blur_scale * (mass - (high + jnp.log(total)))

    def col_turn(t, running):
        high, total = running
        a, b = t // per_row, chosen[t // per_row, t % per_row]
        s = (src_mine[a][:, None] - scores_of(a, b)) / blur_scale
        new_high = jnp.maximum(high[b], jnp.max(s, axis=0))
        new_total = total[b] * jnp.exp(high[b] - new_high) + jnp.sum(
            jnp.exp(s - new_high[None, :]), axis=0
        )
        return high.at[b].set(new_high), total.at[b].set(new_total)

    start = (jnp.full((cc, pts), floor_value), jnp.zeros((cc, pts)))
    high, total = lax.fori_loop(0, per_dev * per_row, col_turn, start)
    top = lax.pmax(high, ("row", "col"))
    total = lax.psum(total * jnp.exp(high - top), ("row", "col"))
    count = log_dst_mass.shape[0]
    last = lax.dynamic_slice_in_dim(top + jnp.log(total), lax.axis_index("col") * count, count, 0)
    return lax.all_gather(src_mine, "col", axis=0, tiled=True), blur_scale * (log_dst_mass - last)


def body(n_col, src_points, dst_points, support, log_src_mass, log_dst_mass, dst_potential):
    per_dev = support.shape[0] // n_col
    count = dst_points.shape[0]
    x_mine = lax.all_to_all(src_points, "col", split_axis=0, concat_axis=1, tiled=True)
    y_some = lax.all_gather(dst_points, "row", axis=1, tiled=True)
    y_all = lax.all_gather(y_some, "col", axis=0, tiled=True)
    g_all = lax.all_gather(dst_potential, "col", axis=0, tiled=True)
    src_mine, part = tiles(per_dev, support, x_mine, y_all, g_all, log_src_mass)
    whole = lax.psum(part, ("row", "col"))
    src_new = lax.all_gather(src_mine, "col", axis=0, tiled=True)
    fine = jnp.all((whole >= col_low) & (whole <= col_top))
    mine = lax.dynamic_slice_in_dim(whole, lax.axis_index("col") * count, count, 0)
    dst_new = blur_scale * (log_dst_mass - (jnp.log(mine) - 2.0 * dst_potential))
    return lax.cond(
        fine,
        lambda: (src_new, dst_new),
        lambda: exact_path(
            per_dev, support, x_mine, y_all, g_all, log_src_mass, log_dst_mass
        ),
    )


def solution(mesh):
    return jax.shard_map(
        functools.partial(body, mesh.shape["col"]),
        mesh=mesh,
        in_specs=(
            P("row", "col", None),
            P("col", "row", None),
            P("row", None),
            P("row", None),
            P("col", None),
            P("col", None),
        ),
        out_specs=(P("row", None), P("col", None)),
        check_vma=False,
    )
```

time: 1470 us -> 1100 us (0.75); the launches traced: 1440 us -> 1100 us
  loops' own time: 675 us -> 129 us
  waiting for transfers between devices: 61.8 us -> 355 us
  local copies, waits for them, and re-layouts: 221 us -> 53.5 us
  other arithmetic: 180 us -> 312 us
  matrix products: 190 us -> 130 us
  blocking collectives: 101 us -> 59 us
  Pallas kernels: 0 us -> 39.6 us
    another operation x2 -> x3, loops' own time: 675 us -> 129 us  [the longest x1 65.1 us: exact_path(): high, total = lax.fori_loop(0, per_dev * per_row, col_turn, start)]
    psum x1 -> x2, waiting for transfers between devices: 32.6 us -> 228 us  [the longest x1 115 us: exact_path(): total = lax.psum(total * jnp.exp(high - top), ('row', 'col'))]
    dynamic_slice x470 -> x129, local copies, waits for them, and re-layouts: 203 us -> 38.7 us  [the longest x32 19.1 us: row_turn(): a, b = (t // per_row, chosen[t // per_row, t % per_row])]
    another operation x0 -> x192, other arithmetic: none -> 129 us
    pmax x1, waiting for transfers between devices: 28.5 us -> 119 us  [exact_path(): top = lax.pmax(high, ('row', 'col'))]
    dot_general x94 -> x64, matrix products: 190 us -> 130 us  [scores_of(): lax.dot_general(x, y, (((0,), (0,)), ((), ())), preferred_element_type=jn...]
    pallas_call x0 -> x1, Pallas kernels: none -> 39.6 us  [tiles(): pl.pallas_call(functools.partial(tile_kernel, per_dev), out_shape=(jax.Sh...]
    pmax x1 -> x0, blocking collectives: 34.3 us -> none  [body(): final_high = lax.pmax(col_high, 'row')]
  transfers between devices with their start and end apart: 3 -> 5, of which waited for: 2 -> 4; matrix products, arithmetic and copies ran while one was open for 0% -> 0% of each run, Pallas kernels for 0% -> 0%
where the time goes in v1:
time: 1100 us
  waiting for transfers between devices  355 us (32%)
  other arithmetic  312 us (28%)
  matrix products  130 us (12%)
  loops' own time  129 us (12%)
  blocking collectives  59 us (5%)
  local copies, waits for them, and re-layouts  53.5 us (5%)
  Pallas kernels  39.6 us (4%)
  between operations  14.5 us (1%)
    dot_general x64, matrix products, scores_of(): lax.dot_general(x, y, (((0,), (0,)), ((), ())), preferred_element_type=jn...  130 us
    another operation x192, other arithmetic  129 us
    pmax x1, waiting for transfers between devices, exact_path(): top = lax.pmax(high, ('row', 'col'))  119 us
    psum x1, waiting for transfers between devices, exact_path(): total = lax.psum(total * jnp.exp(high - top), ('row', 'col'))  115 us
    psum x1, waiting for transfers between devices, body(): whole = lax.psum(part, ('row', 'col'))  112 us
    another operation x1, loops' own time, exact_path(): high, total = lax.fori_loop(0, per_dev * per_row, col_turn, start)  65.1 us
    another operation x1, loops' own time, exact_path(): high, total = lax.fori_loop(0, per_dev * per_row, row_turn, start)  63.9 us
    reduce_sum x64, other arithmetic, scores_of(): jnp.sum(yf * yf, 0)[None, :]  62.7 us
  transfers between devices with their start and end apart: 5, of which 4 were waited for; matrix products, arithmetic and copies ran while one was open for 0% of the time, Pallas kernels for 0%

profile of v1, /device:TPU:0, one launch (start us, length us, event | category | flops | bytes accessed | tf_op | source)
XLA Modules:
  0.0 1096.6 jit_solution(808435629388894264)
XLA Ops:
  7.2 35.4 %all_gather.15 = bf16[4,64,1024]{2,1,0:T(8,128)(2,1)} all-gather(bf16[4,8,1024]{2,1,0:T(8,128)(2,1)} %param.21), channel_id=1, replica_groups=mesh['row'=8,'col'=4] {'row'}, dimensions={1}, use_global_device_ids=true | all-gather | bytes 589824 | tf_op jit(solution)/shard_map/all_gather | solution.py:163
  42.7 3.5 all-to-all-start
  46.2 11.9 %all-gather.1 = f32[4,4,1024]{2,1,0:T(4,128)S(1)} all-gather(f32[1,4,1024]{2,1,0:T(4,128)} %bitcast.94), channel_id=1, replica_groups=mesh['row'=8,'col'=4] {'col'}, dimensions={0}, use_global_device_ids=true | all-gather | bytes 81920 | tf_op jit(solution)/shard_map/all_gather | solution.py:165
  59.6 8.5 all-gather.5.cloned.1.call-done.y_ref
  68.1 39.6 %tiles.1 = (f32[4,1024]{1,0:T(4,128)}, f32[16,1024]{1,0:T(8,128)}) custom-call(s32[16,8]{1,0:T(8,128)} %copy.16.sup_ref, bf16[4,64,1024]{2,1,0:T(8,128)(2,1)S(1)} %bitcast.79, bf16[16,64,1024]{2,1,0:T(8,128)(2,1)} %all-gather.5.cloned.1.call-done.y_ref, f32[16,1024]{1,0:T(8,128)S(1)} %reshape.239.g_ref, f32[16,1024]{1,0:T(8,128)} %mass_ref.1), custom_call_target="tpu_custom_call" | custom-call | tf_op jit(solution)/shard_map/tiles/pallas_call | solution.py:93
  107.7 5.5 all-gather.2
  113.2 112.3 %all-reduce.8.cloned.1.call-done = f32[16,1024]{1,0:T(8,128)} async-done(((f32[16,1024]{1,0:T(8,128)}), f32[16,1024]{1,0:T(8,128)}) %all-reduce.8.cloned.1.call-update) | async-done | bytes 65552 | tf_op jit(solution)/shard_map/psum | solution.py:167
  227.7 862.4 %conditional.1 = (f32[16,1024]{1,0:T(8,128)}, f32[4,1024]{1,0:T(4,128)}) conditional(s32[]{:T(128)} %convert_element_type.43, (f32[16,1024]{1,0:T(8,128)}, s32[16,8]{0,1:T(8,128)S(1)}, f32[16,1024]{1,0:T(8,128)S(1)}, bf16[4,64,1024]{2,1,0:T(8,128)(2,1)S(1)}, bf16[16,64,1024]{2,1,0:T(8,128)(2,1)}, /*index=5*/f32[4,1024]{1,0:T(4,128)S(1)}) %tuple.177, ...), branch_computations={%region_2.19_spmd, %region_19.20_spmd} | conditional | flops 296581184 | bytes 19873500 | solution.py:172
  227.9 308.2 %while.36 = (s32[]{:T(128)}, f32[4,1024]{1,0:T(4,128)S(1)}, f32[4,1024]{1,0:T(4,128)S(1)}, s32[4,8]{1,0:T(4,128)S(1)}, f32[16,1024]{1,0:T(8,128)S(1)}, /*index=5...) while((s32[]{:T(128)}, f32[4,1024]{1,0:T(4,128)S(1)}, ...), condition=%wide.region_9.9_spmd, body=%wide.region_3.8_spmd.sunk | while | flops 148246560 | bytes 9032689 | solution.py:137
  231.4 2.1 fusion.22
  250.7 2.1 fusion.22
  260.3 2.1 fusion.22
  269.9 2.1 fusion.22
  308.5 2.1 fusion.22
  347.0 2.1 fusion.22
  375.9 2.1 fusion.22
  385.5 2.1 fusion.22
  424.0 2.1 fusion.22
  462.6 2.1 fusion.22
  501.1 2.1 fusion.22
  536.9 308.7 %while.37 = (s32[]{:T(128)}, f32[16,1024]{1,0:T(8,128)S(1)}, f32[16,1024]{1,0:T(8,128)S(1)}, s32[4,8]{1,0:T(4,128)S(1)}, f32[4,1024]{1,0:T(4,128)S(1)}, /*index=...) while((s32[]{:T(128)}, f32[16,1024]{1,0:T(8,128)S(1)}, ...), condition=%wide.region_16.16_spmd, body=%wide.region_10.15_spmd.sunk | while | flops 148244512 | bytes 9020341 | solution.py:151
  846.4 118.5 %all-reduce.4.cloned.1.call-done = f32[16,1024]{1,0:T(8,128)} async-done(((f32[16,1024]{1,0:T(8,128)}), f32[16,1024]{1,0:T(8,128)}) %all-reduce.4.cloned.1.call-update) | async-done | bytes 65552 | tf_op jit(solution)/shard_map/cond/branch_0_fun/pmax | solution.py:152
  966.4 6.3 all-gather
  973.3 115.4 %all-reduce.6.cloned.1.call-done = f32[16,1024]{1,0:T(8,128)} async-done(((f32[16,1024]{1,0:T(8,128)}), f32[16,1024]{1,0:T(8,128)}) %all-reduce.6.cloned.1.call-update) | async-done | bytes 65552 | tf_op jit(solution)/shard_map/cond/branch_0_fun/psum | solution.py:153
  (758 shorter events, 473.0 us)
Async XLA Ops:
  7.2 220.5 %copy-start.1 = (f32[4,1024]{1,0:T(4,128)S(1)}, f32[4,1024]{1,0:T(4,128)}, u32[]{:S(2)}) copy-start(f32[4,1024]{1,0:T(4,128)} %param.25) | copy-start | bytes 49156
  7.2 220.5 %copy-start.3 = (s32[16,8]{0,1:T(8,128)S(1)}, s32[16,8]{0,1:T(8,128)}, u32[]{:S(2)}) copy-start(s32[16,8]{0,1:T(8,128)} %param.22) | copy-start | bytes 1540
  7.2 220.5 %copy-start.2 = (f32[4,1024]{1,0:T(4,128)S(1)}, f32[4,1024]{1,0:T(4,128)}, u32[]{:S(2)}) copy-start(f32[4,1024]{1,0:T(4,128)} %param.24) | copy-start | bytes 49156
  7.2 60.9 %all-gather.5.cloned.1.call-start = ((), (), s32[]{:S(2)}) async-start(), calls=%async_computation.3 | async-start | bytes 2621440 | tf_op jit(solution)/shard_map/all_gather | solution.py:164
  42.7 16.8 %all-to-all-start = ((bf16[16,16,1024]{2,1,0:T(8,128)(2,1)}), bf16[16,16,1024]{2,1,0:T(8,128)(2,1)S(1)}, u32[]{:S(2)}, u32[]{:S(2)}) async-start(bf16[16,16,1024]{2,1,0:T(8,128)(2,1)} %param.20), calls=%async_computation | async-start | bytes 1048576 | tf_op jit(solution)/shard_map/all_to_all | solution.py:162
  46.2 179.3 %all-reduce.8.cloned.1.call-start = ((), (), s32[]{:S(2)}) async-start(), calls=%async_computation.4 | async-start | bytes 131072 | tf_op jit(solution)/shard_map/psum | solution.py:167
  227.7 737.2 %all-reduce.4.cloned.1.call-start = ((), (), s32[]{:S(2)}) async-start(), calls=%async_computation.1 | async-start | bytes 131072 | tf_op jit(solution)/shard_map/cond/branch_0_fun/pmax | solution.py:152
  227.9 309.1 %copy-start.4 = (s32[2]{0:T(128)S(1)}, s32[2]{0:T(128)}, u32[]{:S(2)}) copy-start(s32[2]{0:T(128)} %constant.472.clone.1) | copy-start | bytes 28 | tf_op jit(solution)/shard_map/cond
  227.9 5.6 copy-start.5
  247.1 5.6 copy-start.5
  256.8 5.6 copy-start.5
  266.4 5.6 copy-start.5
  295.3 5.6 copy-start.5
  304.9 5.6 copy-start.5
  333.8 5.6 copy-start.5
  343.5 5.6 copy-start.5
  372.4 5.6 copy-start.5
  382.0 5.6 copy-start.5
  410.9 5.6 copy-start.5
  420.5 5.6 copy-start.5
  449.4 5.6 copy-start.5
  459.0 5.6 copy-start.5
  497.6 5.6 copy-start.5
  846.3 242.4 %all-reduce.6.cloned.1.call-start = ((), (), s32[]{:S(2)}) async-start(), calls=%async_computation.2 | async-start | bytes 131072 | tf_op jit(solution)/shard_map/cond/branch_0_fun/psum | solution.py:153
  (18 other events, 96.2 us)
Sparse Core Ops, SparseCore 0:
  42.8 25.2 all-gather.4
  107.8 117.6 all-reduce.7
  846.4 118.4 all-reduce.3
  970.3 118.3 all-reduce.5

commit v2 on v1

--- a/solution.py
+++ b/solution.py
@@ -19,15 +19,18 @@
 def tile_kernel(
     per_dev, sup_ref, x_ref, y_ref, g_ref, mass_ref, src_ref, t_ref, yaug, xt, ebuf, acc
 ):
-    cc, dim, pts = y_ref.shape
+    n_col, n_row, count, share, pts = y_ref.shape
+    dim = n_row * share
     per_row = sup_ref.shape[1]
     first = lax.axis_index("col") * per_dev
 
     def prep(b, carry):
-        y = y_ref[b]
-        yf = y.astype(jnp.float32)
+        yf = jnp.concatenate(
+            [y_ref[b // count, r, b % count].astype(jnp.float32) for r in range(n_row)], axis=0
+        )
+        y = yf.astype(jnp.bfloat16)
         sq = jnp.sum(yf * yf, axis=0, keepdims=True)
-        bias = 2.0 * (g_ref[pl.ds(b, 1), :] - sq)
+        bias = 2.0 * (g_ref[b // count, pl.ds(b % count, 1), :] - sq)
         hi = bias.astype(jnp.bfloat16).astype(jnp.float32)
         rest = bias - hi
         mid = rest.astype(jnp.bfloat16).astype(jnp.float32)
@@ -38,11 +41,13 @@
         yaug[b, dim:, :] = extra.astype(jnp.bfloat16)
         return carry
 
-    lax.fori_loop(0, cc, prep, 0)
+    lax.fori_loop(0, n_col * count, prep, 0)
     t_ref[...] = jnp.zeros_like(t_ref)
 
     def cluster(a, carry):
-        xf = x_ref[a].astype(jnp.float32)
+        xf = jnp.concatenate(
+            [x_ref[c, a].astype(jnp.float32) for c in range(n_col)], axis=0
+        )
         x_sq = jnp.sum(xf * xf, axis=0, keepdims=True)
         at = lax.broadcasted_iota(jnp.int32, (128 - dim, pts), 0)
         whole = jnp.concatenate([xf * 4.0, jnp.where(at < 3, 1.0, 0.0)], axis=0)
@@ -77,7 +82,7 @@
         def column(k, carry):
             b = sup_ref[first + a, k]
             got = jnp.dot(w16, ebuf[k], preferred_element_type=jnp.float32)
-            t_ref[pl.ds(b, 1), :] += got[0:1] + got[1:2]
+            t_ref[b // count, pl.ds(b % count, 1), :] += got[0:1] + got[1:2]
             return carry
 
         lax.fori_loop(0, per_row, column, 0)
@@ -87,19 +92,19 @@
 
 
 def tiles(per_dev, support, x_mine, y_all, g_all, log_src_mass):
-    cc, dim, pts = y_all.shape
+    n_col, n_row, count, share, pts = y_all.shape
     per_row = support.shape[1]
     vmem = pl.BlockSpec(memory_space=pltpu.VMEM)
     return pl.pallas_call(
         functools.partial(tile_kernel, per_dev),
         out_shape=(
             jax.ShapeDtypeStruct((per_dev, pts), jnp.float32),
-            jax.ShapeDtypeStruct((cc, pts), jnp.float32),
+            jax.ShapeDtypeStruct((n_col, count, pts), jnp.float32),
         ),
         in_specs=[pl.BlockSpec(memory_space=pltpu.SMEM), vmem, vmem, vmem, vmem],
         out_specs=(vmem, vmem),
         scratch_shapes=[
-            pltpu.VMEM((cc, AUG, pts), jnp.bfloat16),
+            pltpu.VMEM((n_col * count, AUG, pts), jnp.bfloat16),
             pltpu.VMEM((pts, 128), jnp.bfloat16),
             pltpu.VMEM((per_row, pts, pts), jnp.bfloat16),
             pltpu.VMEM((pts, 128), jnp.float32),
@@ -110,7 +115,11 @@
 
 
 def exact_path(per_dev, support, x_mine, y_all, g_all, log_src_mass, log_dst_mass):
-    cc, dim, pts = y_all.shape
+    n_col, n_row, count, share, pts = y_all.shape
+    cc, dim = n_col * count, n_row * share
+    x_mine = x_mine.transpose(1, 0, 2, 3).reshape(per_dev, dim, pts)
+    y_all = y_all.transpose(0, 2, 1, 3, 4).reshape(cc, dim, pts)
+    g_all = g_all.reshape(cc, pts)
     per_row = support.shape[1]
     first = lax.axis_index("col") * per_dev
     chosen = lax.dynamic_slice_in_dim(support, first, per_dev, 0)
@@ -151,26 +160,282 @@
     high, total = lax.fori_loop(0, per_dev * per_row, col_turn, start)
     top = lax.pmax(high, ("row", "col"))
     total = lax.psum(total * jnp.exp(high - top), ("row", "col"))
-    count = log_dst_mass.shape[0]
     last = lax.dynamic_slice_in_dim(top + jnp.log(total), lax.axis_index("col") * count, count, 0)
     return lax.all_gather(src_mine, "col", axis=0, tiled=True), blur_scale * (log_dst_mass - last)
 
 
-def body(n_col, src_points, dst_points, support, log_src_mass, log_dst_mass, dst_potential):
+def remote(src, dst, send, recv, row, col):
+    return pltpu.make_async_remote_copy(
+        src_ref=src,
+        dst_ref=dst,
+        send_sem=send,
+        recv_sem=recv,
+        device_id=(row, col),
+        device_id_type=pl.DeviceIdType.MESH,
+    )
+
+
+def greet(n_row, n_col, row, col):
+    barrier = pltpu.get_barrier_semaphore()
+    for j in range(1, n_row):
+        pl.semaphore_signal(
+            barrier,
+            inc=1,
+            device_id=(lax.rem(row + j, n_row), col),
+            device_id_type=pl.DeviceIdType.MESH,
+        )
+    for j in range(1, n_col):
+        pl.semaphore_signal(
+            barrier,
+            inc=1,
+            device_id=(row, lax.rem(col + j, n_col)),
+            device_id_type=pl.DeviceIdType.MESH,
+        )
+    pl.semaphore_wait(barrier, n_row + n_col - 2)
+
+
+def spread_kernel(
+    src_ref, dst_ref, pot_ref, x_ref, y_ref, g_ref, own, x_send, x_recv, g_send, g_recv,
+    row_send, y_send, pair_send, y_recv,
+):
+    n_col, n_row = y_ref.shape[:2]
+    per_dev = x_ref.shape[1]
+    n_y = n_col // 2
+    row, col = lax.axis_index("row"), lax.axis_index("col")
+    pair = col + 1 - 2 * lax.rem(col, 2)
+    kept = (
+        pltpu.make_async_copy(dst_ref, y_ref.at[col, row], own.at[0]),
+        pltpu.make_async_copy(
+            src_ref.at[pl.ds(col * per_dev, per_dev)], x_ref.at[col], own.at[1]
+        ),
+        pltpu.make_async_copy(pot_ref, g_ref.at[col], own.at[2]),
+    )
+    for copy in kept:
+        copy.start()
+    greet(n_row, n_col, row, col)
+
+    def to_row(j):
+        there = lax.rem(row + j, n_row)
+        return remote(
+            dst_ref, y_ref.at[col, row], row_send.at[j], y_recv.at[col, row], there, col
+        )
+
+    def to_y(i, dy):
+        at = lax.rem(row + n_row - i, n_row)
+        block = y_ref.at[col, at]
+        there = lax.rem(col + 2 * dy, n_col)
+        return remote(block, block, y_send.at[dy, i], y_recv.at[col, at], row, there)
+
+    def to_pair(i, dy):
+        at = lax.rem(row + n_row - i, n_row)
+        origin = lax.rem(col + n_col - 2 * dy, n_col)
+        block = y_ref.at[origin, at]
+        return remote(block, block, pair_send.at[dy, i], y_recv.at[origin, at], row, pair)
+
+    def arrived(origin, at):
+        block = y_ref.at[origin, at]
+        remote(block, block, row_send.at[0], y_recv.at[origin, at], row, pair).wait_recv()
+
+    def to_col(j):
+        there = lax.rem(col + j, n_col)
+        return (
+            remote(
+                src_ref.at[pl.ds(there * per_dev, per_dev)],
+                x_ref.at[col], x_send.at[j], x_recv.at[col], row, there,
+            ),
+            remote(pot_ref, g_ref.at[col], g_send.at[j], g_recv.at[col], row, there),
+        )
+
+    for j in range(1, n_row):
+        to_row(j).start()
+    kept[0].wait()
+    for dy in range(1, n_y):
+        to_y(0, dy).start()
+    to_pair(0, 0).start()
+    for j in range(1, n_col):
+        for copy in to_col(j):
+            copy.start()
+
+    def hand_on(i):
+        at = lax.rem(row + n_row - i, n_row)
+        for dy in range(1, n_y):
+            arrived(lax.rem(col + n_col - 2 * dy, n_col), at)
+            to_pair(i, dy).start()
+
+    def step(i, carry):
+        arrived(col, lax.rem(row + n_row - i, n_row))
+        for dy in range(1, n_y):
+            to_y(i, dy).start()
+        to_pair(i, 0).start()
+        hand_on(i - 1)
+        return carry
+
+    lax.fori_loop(1, n_row, step, 0)
+    hand_on(n_row - 1)
+
+    def finish(i, carry):
+        for dy in range(n_y):
+            arrived(lax.rem(pair + 2 * dy, n_col), i)
+            to_pair(i, dy).wait_send()
+            if dy > 0:
+                to_y(i, dy).wait_send()
+        return carry
+
+    lax.fori_loop(0, n_row, finish, 0)
+    for j in range(1, n_row):
+        to_row(j).wait_send()
+    for j in range(1, n_col):
+        for copy in to_col(j):
+            copy.wait_send()
+        origin = lax.rem(col + j, n_col)
+        remote(
+            x_ref.at[origin], x_ref.at[origin], x_send.at[j], x_recv.at[origin], row, pair
+        ).wait_recv()
+        remote(
+            g_ref.at[origin], g_ref.at[origin], g_send.at[j], g_recv.at[origin], row, pair
+        ).wait_recv()
+    kept[1].wait()
+    kept[2].wait()
+
+
+def spread(n_row, n_col, src_points, dst_points, dst_potential):
+    sources, dims, pts = src_points.shape
+    per_dev = sources // n_col
+    sem = pltpu.SemaphoreType.DMA
+    anywhere = pl.BlockSpec(memory_space=pl.ANY)
+    return pl.pallas_call(
+        spread_kernel,
+        out_shape=(
+            jax.ShapeDtypeStruct((n_col, per_dev, dims, pts), src_points.dtype),
+            jax.ShapeDtypeStruct((n_col, n_row) + dst_points.shape, dst_points.dtype),
+            jax.ShapeDtypeStruct((n_col,) + dst_potential.shape, jnp.float32),
+        ),
+        in_specs=[anywhere] * 3,
+        out_specs=(anywhere,) * 3,
+        scratch_shapes=[
+            sem((3,)),
+            sem((n_col,)),
+            sem((n_col,)),
+            sem((n_col,)),
+            sem((n_col,)),
+            sem((n_row,)),
+            sem((n_col // 2, n_row)),
+            sem((n_col // 2, n_row)),
+            sem((n_col, n_row)),
+        ],
+        compiler_params=pltpu.CompilerParams(collective_id=0, has_side_effects=True),
+        name="spread",
+    )(src_points, dst_points, dst_potential)
+
+
+def merge_kernel(
+    part_ref, src_ref, mass_ref, pot_ref, new_src, new_dst, bad_ref, by_col, by_row, srcs, bads,
+    part_send, part_recv, src_send, src_recv, row_send, row_recv, bad_send, bad_recv,
+):
+    n_col = by_col.shape[0]
+    n_row = by_row.shape[0]
+    per_dev = src_ref.shape[0]
+    row, col = lax.axis_index("row"), lax.axis_index("col")
+    greet(n_row, n_col, row, col)
+    started = []
+    for j in range(1, n_col):
+        there = lax.rem(col + j, n_col)
+        started.append(
+            remote(
+                part_ref.at[there], by_col.at[col], part_send.at[j], part_recv.at[col], row, there
+            )
+        )
+        started[-1].start()
+    for j in range(1, n_col):
+        there = lax.rem(col + j, n_col)
+        started.append(
+            remote(src_ref, srcs.at[col], src_send.at[j], src_recv.at[col], row, there)
+        )
+        started[-1].start()
+    by_col[col] = part_ref[col]
+    srcs[col] = src_ref[...]
+
+    def arrivals(held, sems, me, count):
+        for j in range(1, count):
+            at = lax.rem(me + j, count)
+            near = lax.rem(col + 1, n_col)
+            remote(held.at[at], held.at[at], bad_send.at[0], sems.at[at], row, near).wait_recv()
+
+    arrivals(by_col, part_recv, col, n_col)
+    total = by_col[0]
+    for c in range(1, n_col):
+        total = total + by_col[c]
+    by_row[row] = total
+    for j in range(1, n_row):
+        there = lax.rem(row + j, n_row)
+        block = by_row.at[row]
+        started.append(remote(block, block, row_send.at[j], row_recv.at[row], there, col))
+        started[-1].start()
+    arrivals(srcs, src_recv, col, n_col)
+    for c in range(n_col):
+        new_src[c * per_dev : (c + 1) * per_dev, :] = srcs[c]
+    arrivals(by_row, row_recv, row, n_row)
+    total = by_row[0]
+    for r in range(1, n_row):
+        total = total + by_row[r]
+    bad = jnp.where((total >= col_low) & (total <= col_top), 0.0, 1.0)
+    bad = jnp.max(jnp.max(bad, axis=1, keepdims=True), axis=0, keepdims=True)
+    bads[col] = jnp.broadcast_to(bad, bads.shape[1:])
+    for j in range(1, n_col):
+        there = lax.rem(col + j, n_col)
+        block = bads.at[col]
+        started.append(remote(block, block, bad_send.at[j], bad_recv.at[col], row, there))
+        started[-1].start()
+    new_dst[...] = blur_scale * (mass_ref[...] - (jnp.log(total) - 2.0 * pot_ref[...]))
+    arrivals(bads, bad_recv, col, n_col)
+    worst = bads[0]
+    for c in range(1, n_col):
+        worst = jnp.maximum(worst, bads[c])
+    bad_ref[...] = worst
+    for copy in started:
+        copy.wait_send()
+
+
+def merge(n_row, part, src_mine, log_dst_mass, dst_potential):
+    n_col, count, pts = part.shape
+    per_dev = src_mine.shape[0]
+    sem = pltpu.SemaphoreType.DMA
+    vmem = pl.BlockSpec(memory_space=pltpu.VMEM)
+    return pl.pallas_call(
+        merge_kernel,
+        out_shape=(
+            jax.ShapeDtypeStruct((n_col * per_dev, pts), jnp.float32),
+            jax.ShapeDtypeStruct((count, pts), jnp.float32),
+            jax.ShapeDtypeStruct((8, 128), jnp.float32),
+        ),
+        in_specs=[vmem] * 4,
+        out_specs=(vmem,) * 3,
+        scratch_shapes=[
+            pltpu.VMEM((n_col, count, pts), jnp.float32),
+            pltpu.VMEM((n_row, count, pts), jnp.float32),
+            pltpu.VMEM((n_col, per_dev, pts), jnp.float32),
+            pltpu.VMEM((n_col, 8, 128), jnp.float32),
+            sem((n_col,)),
+            sem((n_col,)),
+            sem((n_col,)),
+            sem((n_col,)),
+            sem((n_row,)),
+            sem((n_row,)),
+            sem((n_col,)),
+            sem((n_col,)),
+        ],
+        compiler_params=pltpu.CompilerParams(collective_id=1, has_side_effects=True),
+        name="merge",
+    )(part, src_mine, log_dst_mass, dst_potential)
+
+
+def body(n_row, n_col, src_points, dst_points, support, log_src_mass, log_dst_mass, dst_potential):
     per_dev = support.shape[0] // n_col
-    count = dst_points.shape[0]
-    x_mine = lax.all_to_all(src_points, "col", split_axis=0, concat_axis=1, tiled=True)
-    y_some = lax.all_gather(dst_points, "row", axis=1, tiled=True)
-    y_all = lax.all_gather(y_some, "col", axis=0, tiled=True)
-    g_all = lax.all_gather(dst_potential, "col", axis=0, tiled=True)
+    x_mine, y_all, g_all = spread(n_row, n_col, src_points, dst_points, dst_potential)
     src_mine, part = tiles(per_dev, support, x_mine, y_all, g_all, log_src_mass)
-    whole = lax.psum(part, ("row", "col"))
-    src_new = lax.all_gather(src_mine, "col", axis=0, tiled=True)
-    fine = jnp.all((whole >= col_low) & (whole <= col_top))
-    mine = lax.dynamic_slice_in_dim(whole, lax.axis_index("col") * count, count, 0)
-    dst_new = blur_scale * (log_dst_mass - (jnp.log(mine) - 2.0 * dst_potential))
+    src_new, dst_new, bad = merge(n_row, part, src_mine, log_dst_mass, dst_potential)
     return lax.cond(
-        fine,
+        bad[0, 0] < 0.5,
         lambda: (src_new, dst_new),
         lambda: exact_path(
             per_dev, support, x_mine, y_all, g_all, log_src_mass, log_dst_mass
@@ -180,7 +445,7 @@
 
 def solution(mesh):
     return jax.shard_map(
-        functools.partial(body, mesh.shape["col"]),
+        functools.partial(body, mesh.shape["row"], mesh.shape["col"]),
         mesh=mesh,
         in_specs=(
             P("row", "col", None),

time: 1100 us -> 1070 us (0.973)
  waiting for transfers between devices: 355 us -> 234 us
  matrix products: 130 us -> 188 us
  blocking collectives: 59 us -> 6.25 us
  Pallas kernels: 39.6 us -> 82.8 us
  other arithmetic: 312 us -> 348 us
    psum x1 -> x0, waiting for transfers between devices: 112 us -> none  [body(): whole = lax.psum(part, ('row', 'col'))]
    dot_general x64, matrix products: 130 us -> 188 us  [scores_of(): lax.dot_general(x, y, (((0,), (0,)), ((), ())), preferred_element_type=jn...]
    all_gather x3 -> x0, blocking collectives: 52.8 us -> none  [the longest x1 35.4 us: body(): y_some = lax.all_gather(dst_points, 'row', axis=1, tiled=True)]
    pallas_call x0 -> x2, Pallas kernels: none -> 43.9 us  [the longest x1 29.5 us: spread(): pl.pallas_call(spread_kernel, out_shape=(jax.ShapeDtypeStruct((n_col, per...]
    reduce_sum x32, other arithmetic: 57.3 us -> 100 us  [row_turn(): jnp.sum(jnp.exp(s - new_high[:, None]), axis=1)]
  transfers between devices with their start and end apart: 5 -> 2, of which waited for: 4 -> 2; matrix products, arithmetic and copies ran while one was open for 0% -> 0% of each run, Pallas kernels for 0% -> 0%
where the time goes in v2:
time: 1070 us; the launch traced here: 1060 us
  other arithmetic  348 us (33%)
  waiting for transfers between devices  234 us (22%)
  matrix products  188 us (18%)
  loops' own time  126 us (12%)
  Pallas kernels  82.8 us (8%)
  local copies, waits for them, and re-layouts  59.2 us (6%)
  between operations  14.7 us (1%)
    dot_general x64, matrix products, scores_of(): lax.dot_general(x, y, (((0,), (0,)), ((), ())), preferred_element_type=jn...  188 us
    another operation x192, other arithmetic  124 us
    pmax x1, waiting for transfers between devices, exact_path(): top = lax.pmax(high, ('row', 'col'))  117 us
    psum x1, waiting for transfers between devices, exact_path(): total = lax.psum(total * jnp.exp(high - top), ('row', 'col'))  117 us
    reduce_sum x32, other arithmetic, row_turn(): jnp.sum(jnp.exp(s - new_high[:, None]), axis=1)  100 us
    another operation x1, loops' own time, exact_path(): high, total = lax.fori_loop(0, per_dev * per_row, row_turn, start)  69.3 us
    reduce_sum x64, other arithmetic, scores_of(): jnp.sum(yf * yf, 0)[None, :]  62.5 us
    reduce_sum x32, other arithmetic, col_turn(): jnp.sum(jnp.exp(s - new_high[None, :]), axis=0)  57.6 us
  transfers between devices with their start and end apart: 2, of which 2 were waited for; matrix products, arithmetic and copies ran while one was open for 0% of the time, Pallas kernels for 0%

profile of v2, /device:TPU:0, one launch (start us, length us, event | category | flops | bytes accessed | tf_op | source)
XLA Modules:
  0.0 1058.6 jit_solution(13748598263763807800)
XLA Ops:
  8.5 29.5 %spread.1 = (bf16[4,4,16,1024]{3,2,1,0:T(8,128)(2,1)S(1)}, bf16[4,8,4,8,1024]{4,3,2,1,0:T(8,128)(2,1)S(1)}, f32[4,4,1024]{2,1,0:T(4,128)S(1)}) custom-call(bf16[16,16,1024]{2,1,0:T(8,128)(2,1)} %src_ref.1, bf16[4,8,1024]{2,1,0:T(8,128)(2,1)} %dst_ref.1, f32[4,1024]{1,0:T(4,128)} %pot_ref.3), custom_call_target="tpu_custom_call" | custom-call | tf_op jit(solution)/shard_map/spread/pallas_call | solution.py:306
  38.1 38.9 %tiles.1 = (f32[4,1024]{1,0:T(4,128)}, f32[4,4,1024]{2,1,0:T(4,128)}) custom-call(s32[16,8]{1,0:T(8,128)} %copy.16.sup_ref, bf16[4,4,16,1024]{3,2,1,0:T(8,128)(2,1)S(1)} %get-tuple-element.480.x_ref, bf16[4,8,4,8,1024]{4,3,2,1,0:T(8,128)(2,1)S(1)} %get-tuple-element.481.y_ref, f32[4,4,1024]{2,1,0:T(4,128)S(1)} %get-tuple-element.482.g_ref, f32[16,1024]{1,0:T(8,128)} %mass_ref.2), custom_call_target="tpu_custom_call" | custom-call | tf_op jit(solution)/shard_map/tiles/pallas_call | solution.py:98
  77.0 14.4 %merge.1 = (f32[16,1024]{1,0:T(8,128)S(1)}, f32[4,1024]{1,0:T(4,128)S(1)}, f32[8,128]{1,0:T(8,128)}) custom-call(f32[4,4,1024]{2,1,0:T(4,128)} %get-tuple-element.483.part_ref, f32[4,1024]{1,0:T(4,128)} %get-tuple-element.484.src_ref, f32[4,1024]{1,0:T(4,128)} %mass_ref.3, f32[4,1024]{1,0:T(4,128)} %pot_ref.3), custom_call_target="tpu_custom_call" | custom-call | tf_op jit(solution)/shard_map/merge/pallas_call | solution.py:404
  93.2 957.3 %conditional.1 = ((f32[16,1024]{1,0:T(8,128)S(1)}, f32[4,1024]{1,0:T(4,128)S(1)})) conditional(s32[]{:T(128)} %bitcast.23, (f32[16,1024]{1,0:T(8,128)}, s32[16,8]{0,1:T(8,128)}, f32[4,4,1024]{2,1,0:T(4,128)S(1)}, bf16[4,4,16,1024]{3,2,1,0:T(8,128)(2,1)S(1)}, bf16[4,8,4,8,1024]{4,3,2,1,0:T(8,128)(2,1)S(1)}, ...), branch_computations={%region_0.17_spmd, %region_17.18_spmd} | conditional | flops 296581184 | bytes 25313040 | solution.py:437
  95.7 416.9 %while.36 = (s32[]{:T(128)}, f32[4,1024]{1,0:T(4,128)S(1)}, f32[4,1024]{1,0:T(4,128)S(1)}, s32[4,8]{1,0:T(4,128)S(1)}, f32[16,1024]{1,0:T(8,128)S(1)}, /*index=5...) while((s32[]{:T(128)}, f32[4,1024]{1,0:T(4,128)S(1)}, ...), condition=%wide.region_7.7_spmd, body=%wide.region_1.6_spmd.sunk | while | flops 148246560 | bytes 9032637 | solution.py:146
  113.3 3.9 fusion.22
  139.3 3.9 fusion.22
  165.4 3.9 fusion.22
  191.4 3.9 fusion.22
  217.5 3.9 fusion.22
  243.5 3.9 fusion.22
  269.6 3.9 fusion.22
  295.6 3.9 fusion.22
  321.7 3.9 fusion.22
  347.8 3.9 fusion.22
  373.8 3.9 fusion.22
  399.9 3.9 fusion.22
  425.9 3.9 fusion.22
  452.0 3.9 fusion.22
  478.0 3.9 fusion.22
  513.5 293.9 %while.37 = (s32[]{:T(128)}, f32[16,1024]{1,0:T(8,128)S(1)}, f32[16,1024]{1,0:T(8,128)S(1)}, s32[4,8]{1,0:T(4,128)S(1)}, f32[4,1024]{1,0:T(4,128)S(1)}, /*index=...) while((s32[]{:T(128)}, f32[16,1024]{1,0:T(8,128)S(1)}, ...), condition=%wide.region_14.14_spmd, body=%wide.region_8.13_spmd.sunk | while | flops 148244512 | bytes 9020349 | solution.py:160
  808.1 117.2 %all-reduce.3.cloned.1.call-done = f32[16,1024]{1,0:T(8,128)} async-done(((f32[16,1024]{1,0:T(8,128)}), f32[16,1024]{1,0:T(8,128)}) %all-reduce.3.cloned.1.call-update) | async-done | bytes 65552 | tf_op jit(solution)/shard_map/cond/branch_0_fun/pmax | solution.py:161
  926.8 6.3 all-gather
  933.1 116.7 %all-reduce.5.cloned.1.call-done = f32[16,1024]{1,0:T(8,128)} async-done(((f32[16,1024]{1,0:T(8,128)}), f32[16,1024]{1,0:T(8,128)}) %all-reduce.5.cloned.1.call-update) | async-done | bytes 65552 | tf_op jit(solution)/shard_map/cond/branch_0_fun/psum | solution.py:162
  (686 shorter events, 536.4 us)
Async XLA Ops:
  93.2 2.5 copy-start.3
  93.2 832.0 %all-reduce.3.cloned.1.call-start = ((), (), s32[]{:S(2)}) async-start(), calls=%async_computation | async-start | bytes 131072 | tf_op jit(solution)/shard_map/cond/branch_0_fun/pmax | solution.py:161
  95.7 417.7 %copy-start.2 = (s32[2]{0:T(128)S(1)}, s32[2]{0:T(128)}, u32[]{:S(2)}) copy-start(s32[2]{0:T(128)} %constant.457.clone.1) | copy-start | bytes 28 | tf_op jit(solution)/shard_map/cond
  513.4 536.3 %copy-start.1 = (f32[4,1024]{1,0:T(4,128)S(1)}, f32[4,1024]{1,0:T(4,128)}, u32[]{:S(2)}) copy-start(f32[4,1024]{1,0:T(4,128)} %get-tuple-element.467) | copy-start | bytes 49156 | tf_op jit(solution)/shard_map/cond
  807.4 0.6 copy-start
  808.0 241.7 %all-reduce.5.cloned.1.call-start = ((), (), s32[]{:S(2)}) async-start(), calls=%async_computation.1 | async-start | bytes 131072 | tf_op jit(solution)/shard_map/cond/branch_0_fun/psum | solution.py:162
Sparse Core Ops, SparseCore 0:
  808.1 117.0 all-reduce.2
  931.4 118.3 all-reduce.4

commit v3 on v2

--- a/solution.py
+++ b/solution.py
@@ -17,7 +17,7 @@
 
 
 def tile_kernel(
-    per_dev, sup_ref, x_ref, y_ref, g_ref, mass_ref, src_ref, t_ref, yaug, xt, ebuf, acc
+    per_dev, sup_ref, x_ref, y_ref, g_ref, mass_ref, src_ref, t_ref, yaug, xt, ebuf, acc, wbuf
 ):
     n_col, n_row, count, share, pts = y_ref.shape
     dim = n_row * share
@@ -44,7 +44,13 @@
     lax.fori_loop(0, n_col * count, prep, 0)
     t_ref[...] = jnp.zeros_like(t_ref)
 
-    def cluster(a, carry):
+    def add_column(a, k, n):
+        b = sup_ref[first + a, k]
+        cols = slice(n * COLS, (n + 1) * COLS)
+        got = jnp.dot(wbuf[...], ebuf[k, :, cols], preferred_element_type=jnp.float32)
+        t_ref[b // count, pl.ds(b % count, 1), cols] += got[0:1] + got[1:2]
+
+    def cluster(a, carry, after=True):
         xf = jnp.concatenate(
             [x_ref[c, a].astype(jnp.float32) for c in range(n_col)], axis=0
         )
@@ -57,6 +63,8 @@
         def block(k, carry):
             b = sup_ref[first + a, k]
             for n in range(pts // COLS):
+                if after:
+                    add_column(a - 1, k, n)
                 y = yaug[b, :, n * COLS : (n + 1) * COLS]
                 for m in range(pts // ROWS):
                     rows = pl.ds(m * ROWS, ROWS)
@@ -77,18 +85,19 @@
         w = jnp.where(fine, jnp.exp(mass) / total, jnp.nan)
         w_hi = w.astype(jnp.bfloat16).astype(jnp.float32)
         at16 = lax.broadcasted_iota(jnp.int32, (16, pts), 0)
-        w16 = jnp.where(at16 == 0, w_hi, jnp.where(at16 == 1, w - w_hi, 0.0)).astype(jnp.bfloat16)
-
-        def column(k, carry):
-            b = sup_ref[first + a, k]
-            got = jnp.dot(w16, ebuf[k], preferred_element_type=jnp.float32)
-            t_ref[b // count, pl.ds(b % count, 1), :] += got[0:1] + got[1:2]
-            return carry
-
-        lax.fori_loop(0, per_row, column, 0)
+        w16 = jnp.where(at16 == 0, w_hi, jnp.where(at16 == 1, w - w_hi, 0.0))
+        wbuf[...] = w16.astype(jnp.bfloat16)
         return carry
 
-    lax.fori_loop(0, per_dev, cluster, 0)
+    cluster(0, 0, after=False)
+    lax.fori_loop(1, per_dev, cluster, 0)
+
+    def column(k, carry):
+        for n in range(pts // COLS):
+            add_column(per_dev - 1, k, n)
+        return carry
+
+    lax.fori_loop(0, per_row, column, 0)
 
 
 def tiles(per_dev, support, x_mine, y_all, g_all, log_src_mass):
@@ -108,6 +117,7 @@
             pltpu.VMEM((pts, 128), jnp.bfloat16),
             pltpu.VMEM((per_row, pts, pts), jnp.bfloat16),
             pltpu.VMEM((pts, 128), jnp.float32),
+            pltpu.VMEM((16, pts), jnp.bfloat16),
         ],
         compiler_params=pltpu.CompilerParams(vmem_limit_bytes=56 * 1024 * 1024),
         name="tiles",

time: 1070 us -> 1060 us (level)
  no operation moved by 1% of the time
where the time goes in v3:
time: 1060 us; the launch traced here: 1050 us
  other arithmetic  348 us (33%)
  waiting for transfers between devices  234 us (22%)
  matrix products  188 us (18%)
  loops' own time  126 us (12%)
  Pallas kernels  78.6 us (7%)
  local copies, waits for them, and re-layouts  59.2 us (6%)
  between operations  14.7 us (1%)
    dot_general x64, matrix products, scores_of(): lax.dot_general(x, y, (((0,), (0,)), ((), ())), preferred_element_type=jn...  188 us
    another operation x192, other arithmetic  124 us
    pmax x1, waiting for transfers between devices, exact_path(): top = lax.pmax(high, ('row', 'col'))  117 us
    psum x1, waiting for transfers between devices, exact_path(): total = lax.psum(total * jnp.exp(high - top), ('row', 'col'))  117 us
    reduce_sum x32, other arithmetic, row_turn(): jnp.sum(jnp.exp(s - new_high[:, None]), axis=1)  100 us
    another operation x1, loops' own time, exact_path(): high, total = lax.fori_loop(0, per_dev * per_row, row_turn, start)  69.3 us
    reduce_sum x64, other arithmetic, scores_of(): jnp.sum(yf * yf, 0)[None, :]  62.5 us
    reduce_sum x32, other arithmetic, col_turn(): jnp.sum(jnp.exp(s - new_high[None, :]), axis=0)  57.6 us
  transfers between devices with their start and end apart: 2, of which 2 were waited for; matrix products, arithmetic and copies ran while one was open for 0% of the time, Pallas kernels for 0%

profile of v3, /device:TPU:0, one launch (start us, length us, event | category | flops | bytes accessed | tf_op | source)
XLA Modules:
  0.0 1054.5 jit_solution(12107048274921959453)
XLA Ops:
  8.5 29.5 %spread.1 = (bf16[4,4,16,1024]{3,2,1,0:T(8,128)(2,1)S(1)}, bf16[4,8,4,8,1024]{4,3,2,1,0:T(8,128)(2,1)S(1)}, f32[4,4,1024]{2,1,0:T(4,128)S(1)}) custom-call(bf16[16,16,1024]{2,1,0:T(8,128)(2,1)} %src_ref.1, bf16[4,8,1024]{2,1,0:T(8,128)(2,1)} %dst_ref.1, f32[4,1024]{1,0:T(4,128)} %pot_ref.3), custom_call_target="tpu_custom_call" | custom-call | tf_op jit(solution)/shard_map/spread/pallas_call | solution.py:316
  38.1 34.7 %tiles.1 = (f32[4,1024]{1,0:T(4,128)}, f32[4,4,1024]{2,1,0:T(4,128)}) custom-call(s32[16,8]{1,0:T(8,128)} %copy.16.sup_ref, bf16[4,4,16,1024]{3,2,1,0:T(8,128)(2,1)S(1)} %get-tuple-element.480.x_ref, bf16[4,8,4,8,1024]{4,3,2,1,0:T(8,128)(2,1)S(1)} %get-tuple-element.481.y_ref, f32[4,4,1024]{2,1,0:T(4,128)S(1)} %get-tuple-element.482.g_ref, f32[16,1024]{1,0:T(8,128)} %mass_ref.2), custom_call_target="tpu_custom_call" | custom-call | tf_op jit(solution)/shard_map/tiles/pallas_call | solution.py:107
  72.8 14.4 %merge.1 = (f32[16,1024]{1,0:T(8,128)S(1)}, f32[4,1024]{1,0:T(4,128)S(1)}, f32[8,128]{1,0:T(8,128)}) custom-call(f32[4,4,1024]{2,1,0:T(4,128)} %get-tuple-element.483.part_ref, f32[4,1024]{1,0:T(4,128)} %get-tuple-element.484.src_ref, f32[4,1024]{1,0:T(4,128)} %mass_ref.3, f32[4,1024]{1,0:T(4,128)} %pot_ref.3), custom_call_target="tpu_custom_call" | custom-call | tf_op jit(solution)/shard_map/merge/pallas_call | solution.py:414
  89.0 957.4 %conditional.1 = ((f32[16,1024]{1,0:T(8,128)S(1)}, f32[4,1024]{1,0:T(4,128)S(1)})) conditional(s32[]{:T(128)} %bitcast.23, (f32[16,1024]{1,0:T(8,128)}, s32[16,8]{0,1:T(8,128)}, f32[4,4,1024]{2,1,0:T(4,128)S(1)}, bf16[4,4,16,1024]{3,2,1,0:T(8,128)(2,1)S(1)}, bf16[4,8,4,8,1024]{4,3,2,1,0:T(8,128)(2,1)S(1)}, ...), branch_computations={%region_0.17_spmd, %region_17.18_spmd} | conditional | flops 296581184 | bytes 25313040 | solution.py:447
  91.6 416.9 %while.36 = (s32[]{:T(128)}, f32[4,1024]{1,0:T(4,128)S(1)}, f32[4,1024]{1,0:T(4,128)S(1)}, s32[4,8]{1,0:T(4,128)S(1)}, f32[16,1024]{1,0:T(8,128)S(1)}, /*index=5...) while((s32[]{:T(128)}, f32[4,1024]{1,0:T(4,128)S(1)}, ...), condition=%wide.region_7.7_spmd, body=%wide.region_1.6_spmd.sunk | while | flops 148246560 | bytes 9032637 | solution.py:156
  122.1 3.9 fusion.22
  148.2 3.9 fusion.22
  174.2 3.9 fusion.22
  200.3 3.9 fusion.22
  226.3 3.9 fusion.22
  252.4 3.9 fusion.22
  278.4 3.9 fusion.22
  304.5 3.9 fusion.22
  330.6 3.9 fusion.22
  356.6 3.9 fusion.22
  382.7 3.9 fusion.22
  408.7 3.9 fusion.22
  434.8 3.9 fusion.22
  460.8 3.9 fusion.22
  486.9 3.9 fusion.22
  509.3 293.9 %while.37 = (s32[]{:T(128)}, f32[16,1024]{1,0:T(8,128)S(1)}, f32[16,1024]{1,0:T(8,128)S(1)}, s32[4,8]{1,0:T(4,128)S(1)}, f32[4,1024]{1,0:T(4,128)S(1)}, /*index=...) while((s32[]{:T(128)}, f32[16,1024]{1,0:T(8,128)S(1)}, ...), condition=%wide.region_14.14_spmd, body=%wide.region_8.13_spmd.sunk | while | flops 148244512 | bytes 9020349 | solution.py:170
  803.9 117.2 %all-reduce.3.cloned.1.call-done = f32[16,1024]{1,0:T(8,128)} async-done(((f32[16,1024]{1,0:T(8,128)}), f32[16,1024]{1,0:T(8,128)}) %all-reduce.3.cloned.1.call-update) | async-done | bytes 65552 | tf_op jit(solution)/shard_map/cond/branch_0_fun/pmax | solution.py:171
  922.6 6.3 all-gather
  928.9 116.7 %all-reduce.5.cloned.1.call-done = f32[16,1024]{1,0:T(8,128)} async-done(((f32[16,1024]{1,0:T(8,128)}), f32[16,1024]{1,0:T(8,128)}) %all-reduce.5.cloned.1.call-update) | async-done | bytes 65552 | tf_op jit(solution)/shard_map/cond/branch_0_fun/psum | solution.py:172
  (686 shorter events, 536.4 us)
Async XLA Ops:
  89.0 2.5 copy-start.3
  89.0 832.0 %all-reduce.3.cloned.1.call-start = ((), (), s32[]{:S(2)}) async-start(), calls=%async_computation | async-start | bytes 131072 | tf_op jit(solution)/shard_map/cond/branch_0_fun/pmax | solution.py:171
  91.5 417.7 %copy-start.2 = (s32[2]{0:T(128)S(1)}, s32[2]{0:T(128)}, u32[]{:S(2)}) copy-start(s32[2]{0:T(128)} %constant.457.clone.1) | copy-start | bytes 28 | tf_op jit(solution)/shard_map/cond
  509.3 536.3 %copy-start.1 = (f32[4,1024]{1,0:T(4,128)S(1)}, f32[4,1024]{1,0:T(4,128)}, u32[]{:S(2)}) copy-start(f32[4,1024]{1,0:T(4,128)} %get-tuple-element.467) | copy-start | bytes 49156 | tf_op jit(solution)/shard_map/cond
  803.2 0.6 copy-start
  803.8 241.7 %all-reduce.5.cloned.1.call-start = ((), (), s32[]{:S(2)}) async-start(), calls=%async_computation.1 | async-start | bytes 131072 | tf_op jit(solution)/shard_map/cond/branch_0_fun/psum | solution.py:172
Sparse Core Ops, SparseCore 0:
  804.0 117.0 all-reduce.2
  927.2 118.3 all-reduce.4
